TPU v7x, 128 devices: a whole 4x4x4 slice. The times are simulated.
128 devices in a mesh: ctx: 8 (over z, core), tp: 8 (over y_lo, x), grp: 2 (over y_hi).
Axes of the slice: x: 4, y: 4 (y_hi: 2, y_lo: 2; y = y_hi * 2 + y_lo), z: 4, core: 2. Of those that a mesh axis runs over, the one named last changes fastest.
Arguments:
- merged_hidden: bfloat16 [8192, 5120], P(('ctx', 'grp')), may hold values from -40 to 40
- counts: int32 [16], replicated, may hold values from 1 to 32, 192 in all
- owner: int32 [16, 32], replicated, may hold values from 0 to 15, as said below
- down_proj: bfloat16 [5120, 8192], P(None, 'tp'), may hold values from -0.078125 to 0.078125
- text_embed: bfloat16 [8192, 8192], P(('ctx', 'grp'), 'tp'), may hold values from -64 to 64
- norm_gain: float32 [8192], replicated, may hold values from 0.1 to 1.9
- w_query: bfloat16 [8192, 4096], P(None, 'tp')
- w_key: bfloat16 [8192, 1024], P(None, 'tp')
- w_value: bfloat16 [8192, 1024], P(None, 'tp'), may hold values from -0.0625 to 0.0625
Outputs:
- attended: bfloat16 [8192, 4096], P(('ctx', 'grp'), 'tp')
Inputs may be any that keep to these rules, and one draw needn't show every extreme that they name: `owner`: for each encoder device, window slot i goes to shard p[i mod (8 * 2)] for a permutation p of the shards drawn for that device, so one device's live windows reach one shard at most 2 times. `counts`: the live windows of all devices number 192.
All inputs are finite; a program needn't handle non-finite values.
Results may differ from a plain program's by a relative error of at most 0.013.
The roundings to bfloat16 on the way count: a program that leaves them out, or rounds other values in their place, can miss the bound.
Values may be sent and summed in bfloat16 or wider, within the bound.
A program may use at most 256 MiB of HBM per device.

v0:
```python
import functools
import math

import jax
import jax.numpy as jnp
from jax import lax
from jax.experimental import pallas as pl
from jax.experimental.pallas import tpu as pltpu
from jax.sharding import PartitionSpec as P

HD = 128
NC = 8
NJ = 2
NK = 4
AHEAD = 3
MESH = pl.DeviceIdType.MESH
NEG = float("-inf")


def layer_kernel(
    merged_in, down_in, text_in, counts_in, owner_in, gain, wq_in, wk_in, wv_in, out,
    merged, down, image_sum, packed, arrived, seq, w, q, kv, ahead_by, m, l, acc,
    in_sem, w_sem, as_sem, ar_sem, gs, gr, ks, kr, fs, fr,
):
    rows, cols = text_in.shape
    shards, wcap = owner_in.shape
    window = rows // wcap
    most = wcap // shards
    part = cols // NJ
    depth = merged.shape[2]
    pair_rows = most * window
    chunk = rows // NC
    half = chunk // 2
    heads = q.shape[1] // chunk
    units = NC * NJ
    ctx = lax.axis_index("ctx")
    tp = lax.axis_index("tp")
    yh = lax.axis_index("grp")
    z, core = lax.div(ctx, 2), lax.rem(ctx, 2)
    yl, x = lax.div(tp, 4), lax.rem(tp, 4)
    rank = ctx * 2 + yh

    def at(dx, dy):
        return lax.rem(yl + dy, 2) * 4 + lax.rem(x + dx, 4)

    to_xp, to_xm, to_yp = {"tp": at(1, 0)}, {"tp": at(3, 0)}, {"tp": at(0, 1)}
    sibling = {"ctx": z * 2 + 1 - core}

    def shard_at(step):
        d = lax.rem(rank + step, shards)
        return d, {"ctx": lax.div(d, 2), "grp": lax.rem(d, 2)}

    barrier = pltpu.get_barrier_semaphore()
    partners = [to_xp, to_xm, to_yp] + [shard_at(n)[1] for n in range(1, shards)]
    for dev in partners:
        pl.semaphore_signal(barrier, inc=1, device_id=dev, device_id_type=MESH)

    def col(j):
        return pl.ds(j * part, part)

    loads = []
    for j in range(NJ):
        for k in range(NK):
            deep = pl.ds(k * depth, depth)
            stage = [
                pltpu.make_async_copy(
                    down_in.at[deep, col(j)], down.at[j, k], in_sem.at[j * NK + k]
                )
            ]
            if j == 0:
                stage.append(
                    pltpu.make_async_copy(
                        merged_in.at[:, deep], merged.at[k], in_sem.at[NJ * NK + k]
                    )
                )
            loads.append(stage)
    load_text = [
        pltpu.make_async_copy(text_in.at[:, col(j)], seq.at[0, j], in_sem.at[(NJ + 1) * NK + j])
        for j in range(NJ)
    ]
    load_w = [
        pltpu.make_async_copy(wk_in, w.at[:, :, pl.ds(0, HD)], w_sem.at[0]),
        pltpu.make_async_copy(wv_in, w.at[:, :, pl.ds(HD, HD)], w_sem.at[1]),
        pltpu.make_async_copy(wq_in, w.at[:, :, pl.ds(2 * HD, heads * HD)], w_sem.at[2]),
    ]
    loads.append(load_text)
    loads.append(load_w)
    for stage in loads[:3]:
        for c in stage:
            c.start()

    def remote(src, dst, ssem, rsem, dev):
        return pltpu.make_async_remote_copy(
            src_ref=src, dst_ref=dst, send_sem=ssem, recv_sem=rsem,
            device_id=dev, device_id_type=MESH,
        )

    def iota(shape, axis):
        return lax.broadcasted_iota(jnp.int32, shape, axis)

    shard_ids = iota((shards, wcap), 0)
    counts_col = jnp.sum(
        jnp.where(iota((shards, shards), 0) == iota((shards, shards), 1), counts_in[...], 0),
        axis=1, keepdims=True,
    )
    live = iota((shards, wcap), 1) < counts_col
    owner = owner_in[...]
    lane_win = lax.div(iota((wcap, rows), 1), window)
    spread = (lane_win == iota((wcap, rows), 0)).astype(jnp.float32)
    my_owner = jnp.sum(
        jnp.where(live & (shard_ids == rank), owner + 1, 0), axis=0, keepdims=True
    ).astype(jnp.float32)
    my_owner = jnp.broadcast_to(my_owner, (8, wcap))
    lane_owner = jnp.dot(my_owner, spread, preferred_element_type=jnp.float32)[:1].astype(jnp.int32)
    lane = iota((1, rows), 1)
    lane_slot = lax.div(lane, window * shards)
    slot_row = jnp.where(
        lane_owner > 0,
        (lane_owner - 1) * pair_rows + lane_slot * window + lax.rem(lane, window),
        -1,
    )
    arrivals = jnp.sum(
        (live & (owner == rank)).astype(jnp.int32), axis=1, keepdims=True
    )
    from_shard = lax.div(iota((shards, rows), 1), pair_rows)
    by_shard = iota((shards, rows), 0)
    before = jnp.sum(jnp.where(by_shard < from_shard, arrivals, 0), axis=0, keepdims=True)
    here = jnp.sum(jnp.where(by_shard == from_shard, arrivals, 0), axis=0, keepdims=True)
    pair_slot = lax.div(lax.rem(lane, pair_rows), window)
    dest_row = jnp.where(
        pair_slot < here, (before + pair_slot) * window + lax.rem(lane, window), -1
    )
    filled = jnp.sum(arrivals, axis=0, keepdims=True) * window
    row_ids = iota((rows, rows), 0)
    select = (row_ids == slot_row).astype(jnp.float32).astype(jnp.bfloat16)
    place = (row_ids == dest_row).astype(jnp.float32).astype(jnp.bfloat16)
    is_image = iota((rows, part), 0) < filled

    key = iota(ahead_by.shape, 1)
    dc, dy = lax.div(key, 2 * chunk), lax.rem(lax.div(key, chunk), 2)
    peer = jnp.where(dc == 0, core, 1 - core) * 2 + jnp.where(dy == 0, yh, 1 - yh)
    ahead_by[...] = (
        (peer - core * 2 - yh) * rows + lax.rem(key, chunk)
        - lax.rem(iota(ahead_by.shape, 0), chunk)
    )
    m[...] = jnp.full(m.shape, NEG, jnp.float32)
    l[...] = jnp.zeros(l.shape, jnp.float32)
    acc[...] = jnp.zeros(acc.shape, jnp.float32)

    def project_image(j):
        for k in range(NK):
            for c in loads[j * NK + k]:
                c.wait()
            if j * NK + k + 3 < len(loads):
                for c in loads[j * NK + k + 3]:
                    c.start()
            term = jnp.dot(merged[k], down[j, k], preferred_element_type=jnp.float32)
            if k == 0:
                image_sum[...] = term
            elif k < NK - 1:
                image_sum[...] += term
        image = (image_sum[...] + term).astype(jnp.bfloat16)
        packed[j] = jnp.dot(select, image, preferred_element_type=jnp.float32).astype(
            jnp.bfloat16
        )

    def own_pair():
        return pl.ds(pl.multiple_of(rank * pair_rows, pair_rows), pair_rows)

    a_moves = []

    def send_windows(j):
        for n in range(1, shards):
            d, dev = shard_at(n)
            there = pl.ds(pl.multiple_of(d * pair_rows, pair_rows), pair_rows)
            c = remote(
                packed.at[j, there], arrived.at[j, own_pair()], as_sem.at[j, n], ar_sem.at[j], dev
            )
            c.start()
            a_moves.append(c)
        arrived[j, own_pair(), :] = packed[j, own_pair(), :]

    def place_windows(j):
        others = pl.ds(0, (shards - 1) * pair_rows)
        remote(
            packed.at[j, others], arrived.at[j, others], as_sem.at[j, 0], ar_sem.at[j], sibling
        ).wait_recv()
        load_text[j].wait()
        placed = jnp.dot(place, arrived[j], preferred_element_type=jnp.float32)
        seq[0, j] = jnp.where(is_image, placed, seq[0, j].astype(jnp.float32)).astype(
            jnp.bfloat16
        )

    hops = {
        "own_y": (0, 3, 0, chunk, to_yp, 0),
        "own_xp": (0, 1, 0, chunk, to_xp, 1),
        "own_xm": (0, 2, 0, chunk, to_xm, 2),
        "opp_a": (1, 6, 0, half, to_xp, 3),
        "opp_b": (2, 6, half, half, to_xm, 4),
        "mate_xp": (3, 4, 0, chunk, to_xp, 5),
        "mate_xm": (3, 5, 0, chunk, to_xm, 6),
        "opp_y": (6, 7, 0, chunk, to_yp, 7),
    }

    def hop(u, name):
        src, dst, start, size, dev, index = hops[name]
        i, j = lax.div(u, NJ), lax.rem(u, NJ)
        r = pl.ds(pl.multiple_of(i * chunk + start, 16), size)
        return remote(
            seq.at[src, j, r], seq.at[dst, j, r], gs.at[u, index], gr.at[u, index], dev
        )

    def first(u):
        hop(u, "own_y").start()
        hop(u, "own_xp").start()
        hop(u, "own_xm").start()

    def second(u):
        hop(u, "own_xp").wait_recv()
        hop(u, "opp_a").start()
        hop(u, "own_xm").wait_recv()
        hop(u, "opp_b").start()
        hop(u, "own_y").wait_recv()
        hop(u, "mate_xp").start()
        hop(u, "mate_xm").start()

    def third(u):
        hop(u, "opp_a").wait_recv()
        hop(u, "opp_b").wait_recv()
        hop(u, "opp_y").start()

    places = [(0, 0), (3, 0), (1, 0), (0, 1), (3, 1), (1, 1), (2, 0), (2, 1)]

    def cut(dz, dc, dy, size):
        return pl.ds(((dz * 2 + dc) * 2 + dy) * chunk, size)

    def to_z(dz):
        return {"ctx": lax.rem(z + dz, 4) * 2 + core}

    def exchange(i):
        return remote(
            kv.at[i, cut(0, 0, 0, chunk)], kv.at[i, cut(0, 0, 1, chunk)],
            ks.at[i, 0], kr.at[i, 0], {"grp": 1 - yh},
        )

    def onward(i, dz, dy):
        index = 4 * dy + dz
        return remote(
            kv.at[i, cut(0, 0, dy, chunk)], kv.at[i, cut(dz, 0, dy, chunk)],
            ks.at[i, index], kr.at[i, index], to_z(dz),
        )

    def share(i, dz):
        return remote(
            kv.at[i, cut(dz, 0, 0, 2 * chunk)], kv.at[i, cut(dz, 1, 0, 2 * chunk)],
            fs.at[i, dz], fr.at[i, dz], sibling,
        )

    def project(i):
        r = pl.ds(pl.multiple_of(i * chunk, chunk), chunk)
        for j in range(NJ):
            for name in ("mate_xp", "mate_xm", "opp_y"):
                hop(i * NJ + j, name).wait_recv()

        def block(k):
            return jnp.concatenate([seq[k, j, r] for j in range(NJ)], axis=1).astype(jnp.float32)

        total = jnp.zeros((chunk, 128), jnp.float32)
        for k in range(8):
            v = block(k)
            squares = v * v
            for c in range(cols // 128):
                total = total + squares[:, c * 128:(c + 1) * 128]
        scale = lax.rsqrt(jnp.sum(total, axis=1, keepdims=True) / (8 * cols) + 1e-06)
        result = None
        for k in range(8):
            b = at(*places[k])
            g = gain[:, pl.ds(pl.multiple_of(b * cols, cols), cols)]
            normed = (block(k) * scale * g).astype(jnp.bfloat16)
            term = jnp.dot(normed, w[b], preferred_element_type=jnp.float32)
            result = term if result is None else result + term
        kv[i, cut(0, 0, 0, chunk)] = result[:, :2 * HD].astype(jnp.bfloat16)
        exchange(i).start()
        for dz in range(1, 4):
            @pl.when(z + dz <= 3)
            def _():
                onward(i, dz, 0).start()
        for h in range(heads):
            q[i, h * chunk:(h + 1) * chunk] = result[
                :, (h + 2) * HD:(h + 3) * HD
            ].astype(jnp.bfloat16)

    def kv_one(i):
        exchange(i).wait_recv()
        for dz in range(1, 4):
            @pl.when(z + dz <= 3)
            def _():
                onward(i, dz, 1).start()
        share(i, 0).start()

    def kv_two(i):
        for dz in range(1, 4):
            @pl.when(z >= dz)
            def _():
                onward(i, dz, 0).wait_recv()
                onward(i, dz, 1).wait_recv()
                share(i, dz).start()

    def kv_three(i):
        share(i, 0).wait_recv()
        for dz in range(1, 4):
            @pl.when(z >= dz)
            def _():
                share(i, dz).wait_recv()

    scale2 = math.log2(math.e) / math.sqrt(HD)
    tile = 2 * chunk

    def attend_tiles(pairs, keys):
        work = [(a, pl.ds(t * tile, tile), b) for a, b in pairs for t in range(q.shape[1] // tile)]

        def score(n):
            a, r, b = work[n]
            return lax.dot_general(
                q[a, r], kv[b, :keys, :HD], (((1,), (1,)), ((), ())),
                preferred_element_type=jnp.float32,
            )

        def finish(a, r, b, fade, probs):
            acc[a, r] = acc[a, r] * fade + jnp.dot(
                probs, kv[b, :keys, HD:], preferred_element_type=jnp.float32
            )

        coming = score(0)
        pending = None
        for n, (a, r, b) in enumerate(work):
            s = coming
            if n + 1 < len(work):
                coming = score(n + 1)
            cuts = [s[:, c * 128:(c + 1) * 128] for c in range(keys // 128)]
            for c in range(4 * chunk // 128):
                seen = ahead_by[:, c * 128:(c + 1) * 128] <= (a - b) * chunk
                cuts[c] = jnp.where(seen, cuts[c], NEG)
            top = jnp.max(functools.reduce(jnp.maximum, cuts), axis=1, keepdims=True)
            old = m[a, r]
            new = jnp.maximum(old, top)
            m[a, r] = new
            fade = jnp.exp2((old - new) * scale2)
            probs = [jnp.exp2((c - new) * scale2) for c in cuts]
            l[a, r] = l[a, r] * fade + functools.reduce(jnp.add, probs)
            probs = jnp.concatenate([p.astype(jnp.bfloat16) for p in probs], axis=1)
            if pending is not None:
                finish(*pending)
            pending = (a, r, b, fade, probs)
        finish(*pending)

    def attend(i, low, high):
        seen = jnp.minimum(i + 2, NC)

        def pair_of(n):
            column = n < seen
            return jnp.where(column, n, jnp.minimum(i + 1, NC - 1)), jnp.where(column, i, n - seen)

        for level in range(4):
            @pl.when(z == level)
            def _():
                @pl.loop(low, high)
                def _(p):
                    attend_tiles(
                        [pair_of(2 * p), pair_of(2 * p + 1)], (level + 1) * 4 * chunk
                    )

    for j in range(NJ):
        project_image(j)
        if j == 0:
            pl.semaphore_wait(barrier, len(partners))
        send_windows(j)
    early = [u for u in range(AHEAD) if u % NJ == 0]
    late = [u for u in range(AHEAD) if u % NJ]
    place_windows(0)
    for u in early:
        first(u)
    second(0)
    place_windows(1)
    for u in late:
        first(u)
    for c in load_w:
        c.wait()

    @pl.loop(0, 2 * NC + 7)
    def _(s):
        @pl.when(jnp.logical_and(s >= 1, s <= units))
        def _():
            third(s - 1)

        @pl.when(jnp.logical_and(s >= 1, s < units))
        def _():
            second(s)

        @pl.when(s + AHEAD < units)
        def _():
            first(s + AHEAD)

        odd = lax.rem(s, 2) == 1

        def chunk_at(lag):
            return lax.div(s - lag, 2)

        def due(lag, parity):
            return jnp.logical_and(
                parity, jnp.logical_and(s >= lag, s - lag <= 2 * (NC - 1))
            )

        even = jnp.logical_not(odd)

        @pl.when(due(4, even))
        def _():
            kv_one(chunk_at(4))

        @pl.when(due(6, even))
        def _():
            kv_two(chunk_at(6))

        @pl.when(due(3, odd))
        def _():
            project(chunk_at(3))

        @pl.when(due(7, odd))
        def _():
            kv_three(chunk_at(7))

        @pl.when(s >= 7)
        def _():
            i = lax.div(s - 7, 2)
            count = jnp.where(i == NC - 1, NC // 2, i + 1)
            cut_at = lax.div(count + 1, 2)
            attend(i, jnp.where(odd, 0, cut_at), jnp.where(odd, cut_at, count))

    for a in range(NC):
        total = jnp.sum(l[a], axis=1, keepdims=True)
        done = (acc[a] / total).astype(jnp.bfloat16)
        for h in range(heads):
            out[a * chunk:(a + 1) * chunk, h * HD:(h + 1) * HD] = done[h * chunk:(h + 1) * chunk]

    for c in a_moves:
        c.wait_send()

    @pl.loop(0, units)
    def _(u):
        for name in hops:
            hop(u, name).wait_send()

    @pl.loop(0, NC)
    def _(i):
        exchange(i).wait_send()
        share(i, 0).wait_send()
        for dz in range(1, 4):
            @pl.when(z + dz <= 3)
            def _():
                onward(i, dz, 0).wait_send()
                onward(i, dz, 1).wait_send()

            @pl.when(z >= dz)
            def _():
                share(i, dz).wait_send()


def local(merged_hidden, counts, owner, down_proj, text_embed, norm_gain, w_query, w_key, w_value):
    rows, cols = text_embed.shape
    hidden = merged_hidden.shape[1]
    blocks = norm_gain.shape[0] // cols
    q_cols = w_query.shape[1]
    heads = q_cols // HD
    chunk = rows // NC
    any_space = pl.BlockSpec(memory_space=pl.ANY)
    vmem = pl.BlockSpec(memory_space=pltpu.VMEM)
    dma = pltpu.SemaphoreType.DMA
    return pl.pallas_call(
        layer_kernel,
        out_shape=jax.ShapeDtypeStruct((rows, q_cols), jnp.bfloat16),
        in_specs=[any_space] * 3 + [vmem] * 3 + [any_space] * 3,
        out_specs=vmem,
        scratch_shapes=[
            pltpu.VMEM((NK, rows, hidden // NK), jnp.bfloat16),
            pltpu.VMEM((NJ, NK, hidden // NK, cols // NJ), jnp.bfloat16),
            pltpu.VMEM((rows, cols // NJ), jnp.float32),
            pltpu.VMEM((NJ, rows, cols // NJ), jnp.bfloat16),
            pltpu.VMEM((NJ, rows, cols // NJ), jnp.bfloat16),
            pltpu.VMEM((8, NJ, rows, cols // NJ), jnp.bfloat16),
            pltpu.VMEM((blocks, cols, q_cols + 2 * HD), jnp.bfloat16),
            pltpu.VMEM((NC, heads * chunk, HD), jnp.bfloat16),
            pltpu.VMEM((NC, 16 * chunk, 2 * HD), jnp.bfloat16),
            pltpu.VMEM((2 * chunk, 4 * chunk), jnp.int32),
            pltpu.VMEM((NC, heads * chunk, 128), jnp.float32),
            pltpu.VMEM((NC, heads * chunk, 128), jnp.float32),
            pltpu.VMEM((NC, heads * chunk, HD), jnp.float32),
            dma(((NJ + 1) * NK + NJ,)),
            dma((3,)),
            dma((NJ, 16)),
            dma((NJ,)),
            dma((NC * NJ, 8)),
            dma((NC * NJ, 8)),
            dma((NC, 8)),
            dma((NC, 8)),
            dma((NC, 4)),
            dma((NC, 4)),
        ],
        compiler_params=pltpu.CompilerParams(
            collective_id=0, has_side_effects=True, vmem_limit_bytes=60 * 1024 * 1024
        ),
        name="layer",
    )(
        merged_hidden,
        down_proj,
        text_embed,
        counts.reshape(1, -1),
        owner,
        norm_gain.reshape(1, -1),
        w_query.reshape(blocks, cols, q_cols),
        w_key.reshape(blocks, cols, HD),
        w_value.reshape(blocks, cols, HD),
    )


def solution(mesh):
    in_specs = (
        P(("ctx", "grp"), None),
        P(),
        P(),
        P(None, "tp"),
        P(("ctx", "grp"), "tp"),
        P(),
        P(None, "tp"),
        P(None, "tp"),
        P(None, "tp"),
    )
    out_specs = P(("ctx", "grp"), "tp")
    return jax.shard_map(local, mesh=mesh, in_specs=in_specs, out_specs=out_specs, check_vma=False)
```

profile of v0, /device:TPU:96, one launch (start us, length us, event | category | flops | bytes accessed | tf_op | source)
XLA Modules:
  0.0 120.6 jit_solution(14984114074997998824)
XLA Ops:
  0.0 118.7 %layer.1 = bf16[512,512]{1,0:T(8,128)(2,1)} custom-call(bf16[512,5120]{1,0:T(8,128)(2,1)} %merged_in.1, bf16[5120,1024]{1,0:T(8,128)(2,1)} %down_in.1, bf16[512,1024]{1,0:T(8,128)(2,1)} %text_in.1, s32[1,16]{1,0:T(1,128)} %bitcast.9, s32[16,32]{1,0:T(8,128)} %owner_in.1, f32[1,8192]{1,0:T(1,128)} %bitcast.8, bf16[8,1024,512]{2,1,0:T(8,128)(2,1)} %bitcast.5, ...), custom_call_target="tpu_custom_call" | custom-call | tf_op jit(solution)/shard_map/layer/pallas_call | solution.py:478
  118.7 1.9 %copy.11 = bf16[512,512]{1,0:T(8,128)(2,1)} copy(bf16[512,512]{1,0:T(8,128)(2,1)} %layer.1) | data formatting | bytes 1048576
where the time goes:
time: 121 us
  Pallas kernels  119 us (98%)
  local copies, waits for them, and re-layouts  1.87 us (2%)
    pallas_call x1, Pallas kernels, local(): pl.pallas_call(layer_kernel, out_shape=jax.ShapeDtypeStruct((rows, q_cols...  119 us

commit v1 on v0

--- a/solution.py
+++ b/solution.py
@@ -13,12 +13,14 @@
 NJ = 2
 NK = 4
 AHEAD = 3
+LATE = 3
 MESH = pl.DeviceIdType.MESH
 NEG = float("-inf")
+LOWEST = -3e38
 
 
 def layer_kernel(
-    merged_in, down_in, text_in, counts_in, owner_in, gain, wq_in, wk_in, wv_in, out,
+    text_first, merged_in, down_in, text_in, counts_in, owner_in, gain, wq_in, wk_in, wv_in, out,
     merged, down, image_sum, packed, arrived, seq, w, q, kv, ahead_by, m, l, acc,
     in_sem, w_sem, as_sem, ar_sem, gs, gr, ks, kr, fs, fr,
 ):
@@ -33,6 +35,12 @@
     half = chunk // 2
     heads = q.shape[1] // chunk
     units = NC * NJ
+    lead = LATE if text_first else 0
+    placed_rows = rows - lead * chunk
+
+    def row_chunk(i):
+        return lax.rem(i + NC - lead, NC)
+
     ctx = lax.axis_index("ctx")
     tp = lax.axis_index("tp")
     yh = lax.axis_index("grp")
@@ -83,8 +91,11 @@
         pltpu.make_async_copy(wv_in, w.at[:, :, pl.ds(HD, HD)], w_sem.at[1]),
         pltpu.make_async_copy(wq_in, w.at[:, :, pl.ds(2 * HD, heads * HD)], w_sem.at[2]),
     ]
-    loads.append(load_text)
+    loads.append([] if text_first else load_text)
     loads.append(load_w)
+    if text_first:
+        for c in load_text:
+            c.start()
     for stage in loads[:3]:
         for c in stage:
             c.start()
@@ -133,8 +144,8 @@
     filled = jnp.sum(arrivals, axis=0, keepdims=True) * window
     row_ids = iota((rows, rows), 0)
     select = (row_ids == slot_row).astype(jnp.float32).astype(jnp.bfloat16)
-    place = (row_ids == dest_row).astype(jnp.float32).astype(jnp.bfloat16)
-    is_image = iota((rows, part), 0) < filled
+    place = (row_ids == dest_row).astype(jnp.float32).astype(jnp.bfloat16)[:placed_rows]
+    is_image = iota((placed_rows, part), 0) < filled
 
     key = iota(ahead_by.shape, 1)
     dc, dy = lax.div(key, 2 * chunk), lax.rem(lax.div(key, chunk), 2)
@@ -143,7 +154,7 @@
         (peer - core * 2 - yh) * rows + lax.rem(key, chunk)
         - lax.rem(iota(ahead_by.shape, 0), chunk)
     )
-    m[...] = jnp.full(m.shape, NEG, jnp.float32)
+    m[...] = jnp.full(m.shape, LOWEST, jnp.float32)
     l[...] = jnp.zeros(l.shape, jnp.float32)
     acc[...] = jnp.zeros(acc.shape, jnp.float32)
 
@@ -185,11 +196,11 @@
         remote(
             packed.at[j, others], arrived.at[j, others], as_sem.at[j, 0], ar_sem.at[j], sibling
         ).wait_recv()
-        load_text[j].wait()
+        if not text_first:
+            load_text[j].wait()
         placed = jnp.dot(place, arrived[j], preferred_element_type=jnp.float32)
-        seq[0, j] = jnp.where(is_image, placed, seq[0, j].astype(jnp.float32)).astype(
-            jnp.bfloat16
-        )
+        text = seq[0, j, :placed_rows].astype(jnp.float32)
+        seq[0, j, :placed_rows] = jnp.where(is_image, placed, text).astype(jnp.bfloat16)
 
     hops = {
         "own_y": (0, 3, 0, chunk, to_yp, 0),
@@ -205,7 +216,7 @@
     def hop(u, name):
         src, dst, start, size, dev, index = hops[name]
         i, j = lax.div(u, NJ), lax.rem(u, NJ)
-        r = pl.ds(pl.multiple_of(i * chunk + start, 16), size)
+        r = pl.ds(pl.multiple_of(row_chunk(i) * chunk + start, 16), size)
         return remote(
             seq.at[src, j, r], seq.at[dst, j, r], gs.at[u, index], gr.at[u, index], dev
         )
@@ -257,7 +268,7 @@
         )
 
     def project(i):
-        r = pl.ds(pl.multiple_of(i * chunk, chunk), chunk)
+        r = pl.ds(pl.multiple_of(row_chunk(i) * chunk, chunk), chunk)
         for j in range(NJ):
             for name in ("mate_xp", "mate_xm", "opp_y"):
                 hop(i * NJ + j, name).wait_recv()
@@ -339,7 +350,7 @@
                 coming = score(n + 1)
             cuts = [s[:, c * 128:(c + 1) * 128] for c in range(keys // 128)]
             for c in range(4 * chunk // 128):
-                seen = ahead_by[:, c * 128:(c + 1) * 128] <= (a - b) * chunk
+                seen = ahead_by[:, c * 128:(c + 1) * 128] <= (row_chunk(a) - row_chunk(b)) * chunk
                 cuts[c] = jnp.where(seen, cuts[c], NEG)
             top = jnp.max(functools.reduce(jnp.maximum, cuts), axis=1, keepdims=True)
             old = m[a, r]
@@ -361,47 +372,84 @@
             column = n < seen
             return jnp.where(column, n, jnp.minimum(i + 1, NC - 1)), jnp.where(column, i, n - seen)
 
+        fours = lax.div(high - low, 2)
         for level in range(4):
+            keys = (level + 1) * 4 * chunk
+
             @pl.when(z == level)
             def _():
-                @pl.loop(low, high)
-                def _(p):
-                    attend_tiles(
-                        [pair_of(2 * p), pair_of(2 * p + 1)], (level + 1) * 4 * chunk
-                    )
-
-    for j in range(NJ):
-        project_image(j)
-        if j == 0:
-            pl.semaphore_wait(barrier, len(partners))
-        send_windows(j)
-    early = [u for u in range(AHEAD) if u % NJ == 0]
-    late = [u for u in range(AHEAD) if u % NJ]
-    place_windows(0)
-    for u in early:
-        first(u)
-    second(0)
-    place_windows(1)
-    for u in late:
-        first(u)
-    for c in load_w:
-        c.wait()
-
-    @pl.loop(0, 2 * NC + 7)
+                @pl.loop(0, fours)
+                def _(t):
+                    at_pair = 2 * (low + 2 * t)
+                    attend_tiles([pair_of(at_pair + n) for n in range(4)], keys)
+
+                @pl.when(high - low > 2 * fours)
+                def _():
+                    attend_tiles([pair_of(2 * high - 2), pair_of(2 * high - 1)], keys)
+
+    def forwards(s):
+        @pl.when(jnp.logical_and(s >= 1, s <= units))
+        def _():
+            third(s - 1)
+
+        @pl.when(s < units)
+        def _():
+            second(s)
+
+        @pl.when(s + AHEAD < units)
+        def _():
+            first(s + AHEAD)
+
+    if text_first:
+        for c in load_text:
+            c.wait()
+        pl.semaphore_wait(barrier, len(partners))
+        for u in range(AHEAD):
+            first(u)
+        project_image(0)
+        send_windows(0)
+        second(0)
+        first(AHEAD)
+        project_image(1)
+        send_windows(1)
+        third(0)
+        second(1)
+        first(AHEAD + 1)
+        third(1)
+        second(2)
+        for c in load_w:
+            c.wait()
+        place_windows(0)
+        place_windows(1)
+        first(AHEAD + 2)
+    else:
+        for j in range(NJ):
+            project_image(j)
+            if j == 0:
+                pl.semaphore_wait(barrier, len(partners))
+            send_windows(j)
+        early = [u for u in range(AHEAD + 2) if u % NJ == 0]
+        late = [u for u in range(AHEAD + 2) if u % NJ]
+        place_windows(0)
+        for u in early:
+            first(u)
+        second(0)
+        place_windows(1)
+        for u in late:
+            first(u)
+        for c in load_w:
+            c.wait()
+        third(0)
+        second(1)
+        third(1)
+        second(2)
+        first(AHEAD + 2)
+
+    @pl.loop(3, 2 * NC + 6)
     def _(s):
-        @pl.when(jnp.logical_and(s >= 1, s <= units))
-        def _():
-            third(s - 1)
-
-        @pl.when(jnp.logical_and(s >= 1, s < units))
-        def _():
-            second(s)
-
-        @pl.when(s + AHEAD < units)
-        def _():
-            first(s + AHEAD)
-
+        forwards(s)
         odd = lax.rem(s, 2) == 1
+        even = jnp.logical_not(odd)
 
         def chunk_at(lag):
             return lax.div(s - lag, 2)
@@ -411,7 +459,13 @@
                 parity, jnp.logical_and(s >= lag, s - lag <= 2 * (NC - 1))
             )
 
-        even = jnp.logical_not(odd)
+        @pl.when(due(5, odd))
+        def _():
+            kv_two(chunk_at(5))
+
+        @pl.when(due(3, odd))
+        def _():
+            project(chunk_at(3))
 
         @pl.when(due(4, even))
         def _():
@@ -419,28 +473,21 @@
 
         @pl.when(due(6, even))
         def _():
-            kv_two(chunk_at(6))
-
-        @pl.when(due(3, odd))
-        def _():
-            project(chunk_at(3))
-
-        @pl.when(due(7, odd))
-        def _():
-            kv_three(chunk_at(7))
-
-        @pl.when(s >= 7)
-        def _():
-            i = lax.div(s - 7, 2)
+            kv_three(chunk_at(6))
+
+        @pl.when(s >= 6)
+        def _():
+            i = lax.div(s - 6, 2)
             count = jnp.where(i == NC - 1, NC // 2, i + 1)
-            cut_at = lax.div(count + 1, 2)
-            attend(i, jnp.where(odd, 0, cut_at), jnp.where(odd, cut_at, count))
+            half_way = jnp.minimum(2 * lax.div(lax.div(count + 1, 2) + 1, 2), count)
+            attend(i, jnp.where(odd, half_way, 0), jnp.where(odd, count, half_way))
 
     for a in range(NC):
         total = jnp.sum(l[a], axis=1, keepdims=True)
         done = (acc[a] / total).astype(jnp.bfloat16)
+        start = (a + NC - lead) % NC * chunk
         for h in range(heads):
-            out[a * chunk:(a + 1) * chunk, h * HD:(h + 1) * HD] = done[h * chunk:(h + 1) * chunk]
+            out[pl.ds(start, chunk), h * HD:(h + 1) * HD] = done[h * chunk:(h + 1) * chunk]
 
     for c in a_moves:
         c.wait_send()
@@ -465,18 +512,17 @@
                 share(i, dz).wait_send()
 
 
-def local(merged_hidden, counts, owner, down_proj, text_embed, norm_gain, w_query, w_key, w_value):
-    rows, cols = text_embed.shape
-    hidden = merged_hidden.shape[1]
-    blocks = norm_gain.shape[0] // cols
-    q_cols = w_query.shape[1]
+def layer(text_first, *operands):
+    rows, cols = operands[2].shape
+    hidden = operands[0].shape[1]
+    blocks, _, q_cols = operands[6].shape
     heads = q_cols // HD
     chunk = rows // NC
     any_space = pl.BlockSpec(memory_space=pl.ANY)
     vmem = pl.BlockSpec(memory_space=pltpu.VMEM)
     dma = pltpu.SemaphoreType.DMA
     return pl.pallas_call(
-        layer_kernel,
+        functools.partial(layer_kernel, text_first),
         out_shape=jax.ShapeDtypeStruct((rows, q_cols), jnp.bfloat16),
         in_specs=[any_space] * 3 + [vmem] * 3 + [any_space] * 3,
         out_specs=vmem,
@@ -506,10 +552,26 @@
             dma((NC, 4)),
         ],
         compiler_params=pltpu.CompilerParams(
-            collective_id=0, has_side_effects=True, vmem_limit_bytes=60 * 1024 * 1024
+            collective_id=int(text_first), has_side_effects=True, vmem_limit_bytes=60 * 1024 * 1024
         ),
-        name="layer",
-    )(
+        name="layer_text_first" if text_first else "layer",
+    )(*operands)
+
+
+def local(merged_hidden, counts, owner, down_proj, text_embed, norm_gain, w_query, w_key, w_value):
+    rows, cols = text_embed.shape
+    shards, wcap = owner.shape
+    blocks = norm_gain.shape[0] // cols
+    q_cols = w_query.shape[1]
+    live = jnp.arange(wcap, dtype=jnp.int32)[None, :] < counts[:, None]
+    ids = jnp.arange(shards, dtype=jnp.int32)
+    hits = (owner[:, :, None] == ids) & live[:, :, None]
+    fullest = jnp.max(jnp.sum(hits.astype(jnp.int32), axis=(0, 1)))
+    text_first = fullest * (rows // wcap) <= rows - LATE * (rows // NC)
+    return lax.cond(
+        text_first,
+        functools.partial(layer, True),
+        functools.partial(layer, False),
         merged_hidden,
         down_proj,
         text_embed,

time: 121 us -> 117 us (0.967)
  Pallas kernels: 119 us -> 112 us
  other arithmetic: 0 us -> 2.2 us
    pallas_call x1, Pallas kernels: 119 us -> 112 us  [layer(): pl.pallas_call(functools.partial(layer_kernel, text_first), out_shape=jax...]
where the time goes in v1:
time: 117 us
  Pallas kernels  112 us (96%)
  other arithmetic  2.2 us (2%)
    pallas_call x1, Pallas kernels, layer(): pl.pallas_call(functools.partial(layer_kernel, text_first), out_shape=jax...  112 us

profile of v1, /device:TPU:96, one launch (start us, length us, event | category | flops | bytes accessed | tf_op | source)
XLA Modules:
  0.0 116.5 jit_solution(11712665717282350088)
XLA Ops:
  0.0 0.7 iota_compare_fusion.1
  0.7 0.8 convert_reduce_fusion
  1.6 0.6 reduce_max.9
  2.9 112.8 %conditional.1 = (bf16[512,512]{1,0:T(8,128)(2,1)S(1)}) conditional(s32[]{:T(128)} %convert_element_type.7, (bf16[512,5120]{1,0:T(8,128)(2,1)}, bf16[5120,1024]{1,0:T(8,128)(2,1)}, bf16[512,1024]{1,0:T(8,128)(2,1)}, s32[16]{0:T(128)}, s32[16,32]{1,0:T(8,128)}, /*index=5*/f32[8192]{0:T(1024)}, bf16[8192,512]{1,0:T(8,128)(2,1)}, ...), branch_computations={%region_2.0_spmd, %region_3.0_spmd} | conditional | bytes 8 | solution.py:571
  3.1 112.3 %layer_text_first.1 = bf16[512,512]{1,0:T(8,128)(2,1)S(1)} custom-call(bf16[512,5120]{1,0:T(8,128)(2,1)} %get-tuple-element.80.merged_in, bf16[5120,1024]{1,0:T(8,128)(2,1)} %get-tuple-element.82.down_in, bf16[512,1024]{1,0:T(8,128)(2,1)} %get-tuple-element.84.text_in, s32[1,16]{1,0:T(1,128)} %bitcast.19, s32[16,32]{1,0:T(8,128)} %get-tuple-element.57.owner_in, ...), custom_call_target="tpu_custom_call" | custom-call | tf_op jit(solution)/shard_map/cond/branch_1_fun/layer_text_first/pallas_call | solution.py:524
  115.7 0.8 copy.29

commit v2 on v1

--- a/solution.py
+++ b/solution.py
@@ -388,11 +388,11 @@
                     attend_tiles([pair_of(2 * high - 2), pair_of(2 * high - 1)], keys)
 
     def forwards(s):
-        @pl.when(jnp.logical_and(s >= 1, s <= units))
+        @pl.when(s <= units)
         def _():
             third(s - 1)
 
-        @pl.when(s < units)
+        @pl.when(jnp.logical_and(s >= 4, s < units))
         def _():
             second(s)
 
@@ -404,24 +404,22 @@
         for c in load_text:
             c.wait()
         pl.semaphore_wait(barrier, len(partners))
-        for u in range(AHEAD):
+        for u in range(LATE * NJ):
             first(u)
         project_image(0)
         send_windows(0)
         second(0)
-        first(AHEAD)
+        second(1)
         project_image(1)
         send_windows(1)
         third(0)
-        second(1)
-        first(AHEAD + 1)
         third(1)
         second(2)
+        second(3)
         for c in load_w:
             c.wait()
         place_windows(0)
         place_windows(1)
-        first(AHEAD + 2)
     else:
         for j in range(NJ):
             project_image(j)
@@ -444,6 +442,7 @@
         third(1)
         second(2)
         first(AHEAD + 2)
+        second(3)
 
     @pl.loop(3, 2 * NC + 6)
     def _(s):
@@ -459,17 +458,9 @@
                 parity, jnp.logical_and(s >= lag, s - lag <= 2 * (NC - 1))
             )
 
-        @pl.when(due(5, odd))
-        def _():
-            kv_two(chunk_at(5))
-
         @pl.when(due(3, odd))
         def _():
             project(chunk_at(3))
-
-        @pl.when(due(4, even))
-        def _():
-            kv_one(chunk_at(4))
 
         @pl.when(due(6, even))
         def _():
@@ -481,6 +472,14 @@
             count = jnp.where(i == NC - 1, NC // 2, i + 1)
             half_way = jnp.minimum(2 * lax.div(lax.div(count + 1, 2) + 1, 2), count)
             attend(i, jnp.where(odd, half_way, 0), jnp.where(odd, count, half_way))
+
+        @pl.when(due(4, even))
+        def _():
+            kv_one(chunk_at(4))
+
+        @pl.when(due(5, odd))
+        def _():
+            kv_two(chunk_at(5))
 
     for a in range(NC):
         total = jnp.sum(l[a], axis=1, keepdims=True)

time: 117 us -> 110 us (0.940)
  Pallas kernels: 112 us -> 105 us
    pallas_call x1, Pallas kernels: 112 us -> 105 us  [layer(): pl.pallas_call(functools.partial(layer_kernel, text_first), out_shape=jax...]
where the time goes in v2:
time: 110 us; the launch traced here: 109 us
  Pallas kernels  105 us (95%)
  other arithmetic  2.2 us (2%)
    pallas_call x1, Pallas kernels, layer(): pl.pallas_call(functools.partial(layer_kernel, text_first), out_shape=jax...  105 us

profile of v2, /device:TPU:96, one launch (start us, length us, event | category | flops | bytes accessed | tf_op | source)
XLA Modules:
  0.0 109.4 jit_solution(13444626471108998812)
XLA Ops:
  0.0 0.7 iota_compare_fusion.1
  0.7 0.8 convert_reduce_fusion
  1.6 0.6 reduce_max.9
  2.9 105.7 %conditional.1 = (bf16[512,512]{1,0:T(8,128)(2,1)S(1)}) conditional(s32[]{:T(128)} %convert_element_type.7, (bf16[512,5120]{1,0:T(8,128)(2,1)}, bf16[5120,1024]{1,0:T(8,128)(2,1)}, bf16[512,1024]{1,0:T(8,128)(2,1)}, s32[16]{0:T(128)}, s32[16,32]{1,0:T(8,128)}, /*index=5*/f32[8192]{0:T(1024)}, bf16[8192,512]{1,0:T(8,128)(2,1)}, ...), branch_computations={%region_2.0_spmd, %region_3.0_spmd} | conditional | bytes 8 | solution.py:570
  3.1 105.1 %layer_text_first.1 = bf16[512,512]{1,0:T(8,128)(2,1)S(1)} custom-call(bf16[512,5120]{1,0:T(8,128)(2,1)} %get-tuple-element.80.merged_in, bf16[5120,1024]{1,0:T(8,128)(2,1)} %get-tuple-element.82.down_in, bf16[512,1024]{1,0:T(8,128)(2,1)} %get-tuple-element.84.text_in, s32[1,16]{1,0:T(1,128)} %bitcast.19, s32[16,32]{1,0:T(8,128)} %get-tuple-element.57.owner_in, ...), custom_call_target="tpu_custom_call" | custom-call | tf_op jit(solution)/shard_map/cond/branch_1_fun/layer_text_first/pallas_call | solution.py:523
  108.6 0.8 copy.29

commit v3 on v2

--- a/solution.py
+++ b/solution.py
@@ -211,7 +211,16 @@
         "mate_xp": (3, 4, 0, chunk, to_xp, 5),
         "mate_xm": (3, 5, 0, chunk, to_xm, 6),
         "opp_y": (6, 7, 0, chunk, to_yp, 7),
+        "less_xp": (3, 4, 0, chunk - 16, to_xp, 5),
+        "less_xm": (3, 5, 0, chunk - 16, to_xm, 6),
+        "side_a": (1, 4, chunk - 16, 16, to_yp, 8),
+        "side_b": (2, 5, chunk - 16, 16, to_yp, 9),
     }
+    even_hops = [n for n in hops if n not in ("less_xp", "less_xm", "side_a", "side_b")]
+    odd_hops = [n for n in hops if n not in ("mate_xp", "mate_xm")]
+
+    def is_odd(u):
+        return lax.rem(u, 2) == 1
 
     def hop(u, name):
         src, dst, start, size, dev, index = hops[name]
@@ -232,8 +241,18 @@
         hop(u, "own_xm").wait_recv()
         hop(u, "opp_b").start()
         hop(u, "own_y").wait_recv()
-        hop(u, "mate_xp").start()
-        hop(u, "mate_xm").start()
+
+        @pl.when(is_odd(u))
+        def _():
+            hop(u, "less_xp").start()
+            hop(u, "less_xm").start()
+            hop(u, "side_a").start()
+            hop(u, "side_b").start()
+
+        @pl.when(jnp.logical_not(is_odd(u)))
+        def _():
+            hop(u, "mate_xp").start()
+            hop(u, "mate_xm").start()
 
     def third(u):
         hop(u, "opp_a").wait_recv()
@@ -270,7 +289,8 @@
     def project(i):
         r = pl.ds(pl.multiple_of(row_chunk(i) * chunk, chunk), chunk)
         for j in range(NJ):
-            for name in ("mate_xp", "mate_xm", "opp_y"):
+            names = ("less_xp", "less_xm", "side_a", "side_b") if j else ("mate_xp", "mate_xm")
+            for name in names + ("opp_y",):
                 hop(i * NJ + j, name).wait_recv()
 
         def block(k):
@@ -493,8 +513,15 @@
 
     @pl.loop(0, units)
     def _(u):
-        for name in hops:
-            hop(u, name).wait_send()
+        @pl.when(is_odd(u))
+        def _():
+            for name in odd_hops:
+                hop(u, name).wait_send()
+
+        @pl.when(jnp.logical_not(is_odd(u)))
+        def _():
+            for name in even_hops:
+                hop(u, name).wait_send()
 
     @pl.loop(0, NC)
     def _(i):
@@ -543,8 +570,8 @@
             dma((3,)),
             dma((NJ, 16)),
             dma((NJ,)),
-            dma((NC * NJ, 8)),
-            dma((NC * NJ, 8)),
+            dma((NC * NJ, 10)),
+            dma((NC * NJ, 10)),
             dma((NC, 8)),
             dma((NC, 8)),
             dma((NC, 4)),

time: 110 us -> 111 us (level)
  Pallas kernels: 105 us -> 107 us
    pallas_call x1, Pallas kernels: 105 us -> 107 us  [layer(): pl.pallas_call(functools.partial(layer_kernel, text_first), out_shape=jax...]
where the time goes in v3:
time: 111 us
  Pallas kernels  107 us (96%)
  other arithmetic  2.2 us (2%)
    pallas_call x1, Pallas kernels, layer(): pl.pallas_call(functools.partial(layer_kernel, text_first), out_shape=jax...  107 us

profile of v3, /device:TPU:96, one launch (start us, length us, event | category | flops | bytes accessed | tf_op | source)
XLA Modules:
  0.0 111.0 jit_solution(7915149735513507875)
XLA Ops:
  0.0 0.7 iota_compare_fusion.1
  0.7 0.8 convert_reduce_fusion
  1.6 0.6 reduce_max.9
  2.9 107.3 %conditional.1 = (bf16[512,512]{1,0:T(8,128)(2,1)S(1)}) conditional(s32[]{:T(128)} %convert_element_type.7, (bf16[512,5120]{1,0:T(8,128)(2,1)}, bf16[5120,1024]{1,0:T(8,128)(2,1)}, bf16[512,1024]{1,0:T(8,128)(2,1)}, s32[16]{0:T(128)}, s32[16,32]{1,0:T(8,128)}, /*index=5*/f32[8192]{0:T(1024)}, bf16[8192,512]{1,0:T(8,128)(2,1)}, ...), branch_computations={%region_2.0_spmd, %region_3.0_spmd} | conditional | bytes 8 | solution.py:597
  3.1 106.8 %layer_text_first.1 = bf16[512,512]{1,0:T(8,128)(2,1)S(1)} custom-call(bf16[512,5120]{1,0:T(8,128)(2,1)} %get-tuple-element.80.merged_in, bf16[5120,1024]{1,0:T(8,128)(2,1)} %get-tuple-element.82.down_in, bf16[512,1024]{1,0:T(8,128)(2,1)} %get-tuple-element.84.text_in, s32[1,16]{1,0:T(1,128)} %bitcast.19, s32[16,32]{1,0:T(8,128)} %get-tuple-element.57.owner_in, ...), custom_call_target="tpu_custom_call" | custom-call | tf_op jit(solution)/shard_map/cond/branch_1_fun/layer_text_first/pallas_call | solution.py:550
  110.2 0.8 copy.29
